TPU v7x, 32 devices: a whole 2x2x4 slice. The times are simulated.
32 devices in a mesh: groups: 2 (over x), band: 16 (over z, y, core).
Axes of the slice: x: 2, y: 2, z: 4, core: 2. Of those that a mesh axis runs over, the one named last changes fastest.
Arguments:
- factor: bfloat16 [32768, 128], P(('groups', 'band')), parts along dimension 0
- near_vals: bfloat16 [512, 5, 64, 64], P(('groups', 'band')), parts along dimension 0, may hold values from 0.049804688 to 4
- far_vals: bfloat16 [32768, 512], P(('groups', 'band')), parts along dimension 0, may hold values from 0.049804688 to 4
- pub_rows: int32 [32, 32], P(('groups', 'band')), parts along dimension 0, may hold values from 0 to 1023
- far_count: int32 [32, 16], P(('groups', 'band')), parts along dimension 0, may hold values from 1 to 32, as said below
Outputs:
- updated: float32 [32768, 128], P(('groups', 'band')), parts along dimension 0
There are 2 independent parts, one for each index of `groups`. A program takes and returns all parts, laid end to end along the dimension named above; each array names one. Nothing has to cross between parts.
Inputs may be any that keep to these rules, and one draw needn't show every extreme that they name: `far_count`: in every row some entry equals 32.
All inputs are finite; a program needn't handle non-finite values.
Results may differ from a plain program's by a relative error of at most 0.0003.
Values may be sent and summed in bfloat16 or wider, within the bound.
A program may use at most 64 MiB of HBM per device.

v0:
```python
import jax
import jax.numpy as jnp
from jax import lax
from jax.sharding import PartitionSpec as P

BLOCK = 64
HALF_BLOCKS = 2


def extended(shard, sides, width):
    for axis, dim in sides:
        peers, length = (lax.axis_size(axis), shard.shape[dim])
        up = [(i, (i + 1) % peers) for i in range(peers - 1)]
        down = [(j, i) for i, j in up]
        last = lax.slice_in_dim(shard, length - width, length, axis=dim)
        first = lax.slice_in_dim(shard, 0, width, axis=dim)
        before = lax.ppermute(last, axis, up)
        after = lax.ppermute(first, axis, down)
        shard = jnp.concatenate([before, shard, after], axis=dim)
    return shard


def shards(factor, near_vals, far_vals, pub_rows, far_count):
    row_count, rank_width = factor.shape
    band_size = lax.axis_size("band")
    margin = HALF_BLOCKS * BLOCK
    padded = extended(factor, (("band", 0),), margin)
    block_count = row_count // BLOCK
    blocks = padded.reshape(block_count + 2 * HALF_BLOCKS, BLOCK, rank_width)
    near_sum = jnp.zeros((block_count, BLOCK, rank_width), jnp.float32)
    for offset in range(2 * HALF_BLOCKS + 1):
        near_sum = near_sum + jnp.einsum(
            "bij,bjk->bik",
            near_vals[:, offset],
            blocks[offset : offset + block_count],
            preferred_element_type=jnp.float32,
        )
    near_sum = near_sum.reshape(row_count, rank_width)
    slot_count = pub_rows.shape[1]
    chosen = jnp.take(factor, pub_rows[0], axis=0)
    slot_index = jnp.arange(band_size * slot_count, dtype=jnp.int32) % slot_count
    live_slots = slot_index < jnp.repeat(far_count[0], slot_count)
    masked = jnp.where(live_slots[None, :], far_vals, jnp.zeros((), far_vals.dtype))
    own_gram = lax.dot_general(
        factor, factor, (((0,), (0,)), ((), ())), preferred_element_type=jnp.float32
    )
    gram_matrix = lax.psum(own_gram, "band")
    arrived = lax.all_gather(chosen, "band", axis=0, tiled=True)
    far_sum = jnp.dot(masked, arrived, preferred_element_type=jnp.float32)
    lower_factor = jnp.linalg.cholesky(gram_matrix)
    inverse = jax.scipy.linalg.cho_solve(
        (lower_factor, True), jnp.eye(rank_width, dtype=jnp.float32)
    )
    return jnp.dot(near_sum + far_sum, inverse, precision=lax.Precision.HIGHEST)


def solution(mesh):
    placed = (
        P(("groups", "band"), None),
        P(("groups", "band"), None, None, None),
        P(("groups", "band"), None),
        P(("groups", "band"), None),
        P(("groups", "band"), None),
    )
    return jax.shard_map(
        shards, mesh=mesh, in_specs=placed, out_specs=P(("groups", "band"), None), check_vma=False
    )
```

profile of v0, /device:TPU:8, one launch (start us, length us, event | category | flops | bytes accessed | tf_op | source)
XLA Modules:
  0.0 138.6 jit_solution(12282025486069231995)
XLA Ops:
  6.5 0.0 copy-start
  6.5 0.0 all-reduce.2.cloned.1.call-start
  6.5 0.8 fusion.33
  7.4 1.9 %collective-permute-start = (bf16[128,128]{1,0:T(8,128)(2,1)S(1)}, bf16[128,128]{1,0:T(8,128)(2,1)S(1)}, u32[]{:S(2)}, u32[]{:S(2)}) collective-permute-start(bf16[128,128]{1,0:T(8,128)(2,1)S(1)} %get-tuple-element.11), channel_id=1, source_target_pairs={{0,1},{1,2},{2,3},{3,4},{4,5},{5,6},{6,7},{7,8},{8,9},{9,10},{10,1... | collective-permute-start | bytes 98312 | tf_op jit(solution)/shard_map/ppermute | solution.py:17
  9.3 4.5 %collective-permute-start.1 = (bf16[128,128]{1,0:T(8,128)(2,1)S(1)}, bf16[128,128]{1,0:T(8,128)(2,1)S(1)}, u32[]{:S(2)}, u32[]{:S(2)}) collective-permute-start(bf16[128,128]{1,0:T(8,128)(2,1)S(1)} %get-tuple-element.12), channel_id=1, source_target_pairs={{1,0},{2,1},{3,2},{4,3},{5,4},{6,5},{7,6},{8,7},{9,8},{10,9},{11,1... | collective-permute-start | bytes 98312 | tf_op jit(solution)/shard_map/ppermute | solution.py:18
  13.8 1.9 %fusion.34 = f32[128,128]{0,1:T(8,128)} fusion(bf16[1024,128]{1,0:T(8,128)(2,1)} %param.5), kind=kOutput, calls=%fused_computation.56 | convolution fusion | flops 33554432 | bytes 327680 | tf_op jit(solution)/shard_map/dot_general | solution.py:44
  15.8 0.0 all-reduce.2.cloned.1.call-update
  15.8 0.7 fusion.29
  16.5 0.7 compare_and_fusion
  17.1 1.6 %gather_fusion = bf16[32,128]{1,0:T(8,128)(2,1)S(1)} fusion(bf16[1024,128]{1,0:T(8,128)(2,1)} %param.5, s32[1024]{0:T(1024)S(1)} %pad_clamp_fusion), kind=kCustom, calls=%fused_computation | custom fusion | bytes 16512 | tf_op jit(solution)/shard_map/jit(_take)/gather | solution.py:40
  18.7 0.7 broadcast_in_dim.28
  19.4 0.1 reshape.74
  19.5 0.0 copy-start.1
  19.5 1.3 fusion.9
  20.9 0.1 broadcast_select_fusion
  20.9 19.7 %all_gather.3 = bf16[512,128]{1,0:T(8,128)(2,1)} all-gather(bf16[32,128]{1,0:T(8,128)(2,1)S(1)} %broadcast_select_fusion), channel_id=1, replica_groups=mesh['groups'=2,'band'=16] {'band'}, dimensions={0}, use_global_device_ids=true | all-gather | bytes 139264 | tf_op jit(solution)/shard_map/all_gather | solution.py:48
  40.6 0.0 collective-permute-done
  40.6 0.0 copy-done
  40.6 0.1 constant_dynamic-update-slice_fusion
  40.7 0.0 copy-done.1
  40.7 0.2 fusion.11
  40.9 0.0 collective-permute-done.1
  41.0 0.2 convolution_bitcast_fusion
  41.2 62.1 %all-reduce.2.cloned.1.call-done = f32[128,128]{0,1:T(8,128)} async-done(((f32[128,128]{0,1:T(8,128)}), f32[128,128]{0,1:T(8,128)}) %all-reduce.2.cloned.1.call-update) | async-done | bytes 65552 | tf_op jit(solution)/shard_map/psum | solution.py:47
  103.3 0.9 copy.12
  104.2 0.9 fusion.24
  105.1 11.7 %cholesky.17 = f32[128,128]{1,0:T(8,128)S(1)} custom-call(f32[128,128]{1,0:T(8,128)S(1)} %fusion.24), custom_call_target="Cholesky" | custom-call | tf_op jit(solution)/shard_map/jit(cholesky)/cholesky | solution.py:50
  116.8 0.6 compare_reduce_fusion
  117.5 0.7 fusion.19
  118.1 9.8 %custom-call.10 = f32[1,128,128]{1,2,0:T(8,128)S(1)} custom-call(f32[1,128,128]{2,1,0:T(8,128)S(1)} %fusion.19), custom_call_target="InvertDiagBlocksLowerTriangular" | custom-call | tf_op jit(solution)/shard_map/jit(_cho_solve)/triangular_solve | solution.py:51
  128.0 0.2 fusion.22
  128.2 0.2 fusion.20
  128.4 0.2 fusion.3
  128.6 0.0 copy-start.2
  128.7 0.0 copy-start.3
  128.7 0.2 fusion.1
  128.9 0.7 copy-done.2
  129.6 0.4 copy-done.3
  130.0 0.4 convolution_add_fusion
  130.4 1.4 fusion.35
  (7 shorter events, 0.1 us)
Async XLA Ops:
  6.5 34.1 %copy-start = (bf16[1024,128]{1,0:T(8,128)(2,1)S(1)}, bf16[1024,128]{1,0:T(8,128)(2,1)}, u32[]{:S(2)}) copy-start(bf16[1024,128]{1,0:T(8,128)(2,1)} %param.5) | copy-start | bytes 786436
  6.5 96.8 %all-reduce.2.cloned.1.call-start = ((), (), s32[]{:S(2)}) async-start(), calls=%async_computation | async-start | bytes 131072 | tf_op jit(solution)/shard_map/psum | solution.py:47
  7.4 33.2 %collective-permute-start = (bf16[128,128]{1,0:T(8,128)(2,1)S(1)}, bf16[128,128]{1,0:T(8,128)(2,1)S(1)}, u32[]{:S(2)}, u32[]{:S(2)}) collective-permute-start(bf16[128,128]{1,0:T(8,128)(2,1)S(1)} %get-tuple-element.11), channel_id=1, source_target_pairs={{0,1},{1,2},{2,3},{3,4},{4,5},{5,6},{6,7},{7,8},{8,9},{9,10},{10,1... | collective-permute-start | bytes 98312 | tf_op jit(solution)/shard_map/ppermute | solution.py:17
  9.3 31.7 %collective-permute-start.1 = (bf16[128,128]{1,0:T(8,128)(2,1)S(1)}, bf16[128,128]{1,0:T(8,128)(2,1)S(1)}, u32[]{:S(2)}, u32[]{:S(2)}) collective-permute-start(bf16[128,128]{1,0:T(8,128)(2,1)S(1)} %get-tuple-element.12), channel_id=1, source_target_pairs={{1,0},{2,1},{3,2},{4,3},{5,4},{6,5},{7,6},{8,7},{9,8},{10,9},{11,1... | collective-permute-start | bytes 98312 | tf_op jit(solution)/shard_map/ppermute | solution.py:18
  19.5 21.2 %copy-start.1 = (bf16[16,5,64,64]{3,2,1,0:T(8,128)(2,1)S(1)}, bf16[16,5,64,64]{3,2,1,0:T(8,128)(2,1)}, u32[]{:S(2)}) copy-start(bf16[16,5,64,64]{3,2,1,0:T(8,128)(2,1)} %param.6) | copy-start | bytes 1966084
  128.6 0.9 copy-start.2
  128.7 1.3 copy-start.3
Sparse Core Ops, SparseCore 0:
  15.9 87.3 all-reduce.1
where the time goes:
time: 139 us
  waiting for transfers between devices  62.1 us (45%)
  other arithmetic  25.1 us (18%)
  blocking collectives  19.7 us (14%)
  between operations  13.5 us (10%)
  starting transfers between devices  6.45 us (5%)
  matrix products  6.39 us (5%)
  local copies, waits for them, and re-layouts  5.35 us (4%)
    psum x1, waiting for transfers between devices, shards(): gram_matrix = lax.psum(own_gram, 'band')  62.1 us
    all_gather x1, blocking collectives, shards(): arrived = lax.all_gather(chosen, 'band', axis=0, tiled=True)  19.7 us
    another operation x3, other arithmetic, shards(): lower_factor = jnp.linalg.cholesky(gram_matrix)  12.4 us
    another operation x2, other arithmetic, shards(): jax.scipy.linalg.cho_solve((lower_factor, True), jnp.eye(rank_width, dtyp...  10.5 us
    ppermute x1, starting transfers between devices, extended(): after = lax.ppermute(first, axis, down)  4.54 us
  transfers between devices with their start and end apart: 3, of which 1 were waited for; matrix products, arithmetic and copies ran while one was open for 6% of the time, Pallas kernels for 0%

commit v1 on v0

--- a/solution.py
+++ b/solution.py
@@ -44,7 +44,11 @@
     own_gram = lax.dot_general(
         factor, factor, (((0,), (0,)), ((), ())), preferred_element_type=jnp.float32
     )
-    gram_matrix = lax.psum(own_gram, "band")
+    gram_matrix = own_gram
+    for hop in (1, 2, 4, 8):
+        gram_matrix = gram_matrix + lax.ppermute(
+            gram_matrix, "band", [(dev, dev ^ hop) for dev in range(16)]
+        )
     arrived = lax.all_gather(chosen, "band", axis=0, tiled=True)
     far_sum = jnp.dot(masked, arrived, preferred_element_type=jnp.float32)
     lower_factor = jnp.linalg.cholesky(gram_matrix)

time: 139 us -> 76.3 us (0.55)
  the two profiles are of different devices: /device:TPU:8 before, /device:TPU:0 now
where the time goes in v1:
time: 76.3 us; the launch traced here: 76 us
  blocking collectives  25.3 us (33%)
  other arithmetic  24.3 us (32%)
  waiting for transfers between devices  13 us (17%)
  matrix products  5.82 us (8%)
  starting transfers between devices  3.97 us (5%)
  local copies, waits for them, and re-layouts  3.4 us (4%)
    all_gather x1, blocking collectives, shards(): arrived = lax.all_gather(chosen, 'band', axis=0, tiled=True)  25.3 us
    ppermute x4, waiting for transfers between devices, shards(): lax.ppermute(gram_matrix, 'band', [(dev, dev ^ hop) for dev in range(16)])  13 us
    another operation x3, other arithmetic, shards(): lower_factor = jnp.linalg.cholesky(gram_matrix)  12.4 us
    another operation x2, other arithmetic, shards(): jax.scipy.linalg.cho_solve((lower_factor, True), jnp.eye(rank_width, dtyp...  10.5 us
    dot_general x5, matrix products, shards(): jnp.einsum('bij,bjk->bik', near_vals[:, offset], blocks[offset:offset + b...  2.2 us
    ppermute x1, starting transfers between devices, extended(): before = lax.ppermute(last, axis, up)  1.95 us
    gather x1, local copies, waits for them, and re-layouts, shards(): chosen = jnp.take(factor, pub_rows[0], axis=0)  1.57 us
  transfers between devices with their start and end apart: 6, of which 3 were waited for; matrix products, arithmetic and copies ran while one was open for 10% of the time, Pallas kernels for 0%

profile of v1, /device:TPU:0, one launch (start us, length us, event | category | flops | bytes accessed | tf_op | source)
XLA Modules:
  0.0 76.0 jit_solution(3772377194736837126)
XLA Ops:
  0.0 0.0 copy-start
  0.0 1.4 %fusion.34 = f32[128,128]{0,1:T(8,128)S(1)} fusion(bf16[1024,128]{1,0:T(8,128)(2,1)} %param.5), kind=kOutput, calls=%fused_computation.56 | convolution fusion | flops 33554432 | bytes 327680 | tf_op jit(solution)/shard_map/dot_general | solution.py:44
  1.4 0.5 collective-permute-start.2
  1.9 0.8 %fusion.33 = (bf16[128,128]{1,0:T(8,128)(2,1)S(1)}, bf16[128,128]{1,0:T(8,128)(2,1)S(1)}) fusion(bf16[1024,128]{1,0:T(8,128)(2,1)} %param.5), kind=kLoop, calls=%fused_computation.55 | loop fusion | bytes 131072 | tf_op jit(solution)/shard_map/slice | solution.py:15
  2.7 2.0 %collective-permute-start = (bf16[128,128]{1,0:T(8,128)(2,1)S(1)}, bf16[128,128]{1,0:T(8,128)(2,1)S(1)}, u32[]{:S(2)}, u32[]{:S(2)}) collective-permute-start(bf16[128,128]{1,0:T(8,128)(2,1)S(1)} %get-tuple-element.11), channel_id=1, source_target_pairs={{0,1},{1,2},{2,3},{3,4},{4,5},{5,6},{6,7},{7,8},{8,9},{9,10},{10,1... | collective-permute-start | bytes 98312 | tf_op jit(solution)/shard_map/ppermute | solution.py:17
  4.6 1.3 %collective-permute-start.1 = (bf16[128,128]{1,0:T(8,128)(2,1)S(1)}, bf16[128,128]{1,0:T(8,128)(2,1)S(1)}, u32[]{:S(2)}, u32[]{:S(2)}) collective-permute-start(bf16[128,128]{1,0:T(8,128)(2,1)S(1)} %get-tuple-element.12), channel_id=1, source_target_pairs={{1,0},{2,1},{3,2},{4,3},{5,4},{6,5},{7,6},{8,7},{9,8},{10,9},{11,1... | collective-permute-start | bytes 98312 | tf_op jit(solution)/shard_map/ppermute | solution.py:18
  5.9 0.7 fusion.29
  6.6 0.7 compare_and_fusion
  7.3 1.6 %gather_fusion = bf16[32,128]{1,0:T(8,128)(2,1)S(1)} fusion(bf16[1024,128]{1,0:T(8,128)(2,1)} %param.5, s32[1024]{0:T(1024)S(1)} %pad_clamp_fusion), kind=kCustom, calls=%fused_computation | custom fusion | bytes 16512 | tf_op jit(solution)/shard_map/jit(_take)/gather | solution.py:40
  8.8 0.7 broadcast_in_dim.28
  9.6 0.1 reshape.74
  9.7 0.0 copy-start.1
  9.7 1.3 %fusion.9 = f32[16,64,128]{2,1,0:T(8,128)S(1)} fusion(bf16[16,64,128]{2,1,0:T(8,128)(2,1)} %bitcast.72, bf16[16,5,64,64]{3,2,1,0:T(8,128)(2,1)} %param.6), kind=kOutput, calls=%fused_computation.14 | convolution fusion | flops 16777216 | bytes 1048576 | tf_op jit(solution)/shard_map/bij,bjk->bik/dot_general | solution.py:32
  11.0 0.1 broadcast_select_fusion
  11.1 25.3 %all_gather.3 = bf16[512,128]{1,0:T(8,128)(2,1)S(1)} all-gather(bf16[32,128]{1,0:T(8,128)(2,1)S(1)} %broadcast_select_fusion), channel_id=1, replica_groups=mesh['groups'=2,'band'=16] {'band'}, dimensions={0}, use_global_device_ids=true | all-gather | bytes 139264 | tf_op jit(solution)/shard_map/all_gather | solution.py:52
  36.4 0.0 collective-permute-done
  36.4 0.0 copy-done
  36.4 0.1 constant_dynamic-update-slice_fusion
  36.5 0.0 copy-done.1
  36.5 0.2 fusion.11
  36.7 0.2 fusion.3
  36.9 0.0 collective-permute-done.1
  37.0 0.0 collective-permute-done.2
  37.0 0.1 collective-permute-start.3
  37.1 0.2 convolution_bitcast_fusion
  37.3 0.0 copy-start.2
  37.3 4.1 %collective-permute-done.3 = f32[128,128]{0,1:T(8,128)S(1)} collective-permute-done((f32[128,128]{0,1:T(8,128)S(1)}, f32[128,128]{0,1:T(8,128)S(1)}, u32[]{:S(2)}, u32[]{:S(2)}) %collective-permute-start.3) | collective-permute-done | bytes 65568 | tf_op jit(solution)/shard_map/ppermute | solution.py:49
  41.5 0.1 collective-permute-start.4
  41.5 0.2 fusion.1
  41.7 4.0 %collective-permute-done.4 = f32[128,128]{0,1:T(8,128)S(1)} collective-permute-done((f32[128,128]{0,1:T(8,128)S(1)}, f32[128,128]{0,1:T(8,128)S(1)}, u32[]{:S(2)}, u32[]{:S(2)}) %collective-permute-start.4) | collective-permute-done | bytes 65568 | tf_op jit(solution)/shard_map/ppermute | solution.py:49
  45.8 0.1 collective-permute-start.5
  45.9 0.0 copy-done.2
  45.9 0.4 convolution_add_fusion
  46.3 4.8 %collective-permute-done.5 = f32[128,128]{0,1:T(8,128)S(1)} collective-permute-done((f32[128,128]{0,1:T(8,128)S(1)}, f32[128,128]{0,1:T(8,128)S(1)}, u32[]{:S(2)}, u32[]{:S(2)}) %collective-permute-start.5) | collective-permute-done | bytes 65568 | tf_op jit(solution)/shard_map/ppermute | solution.py:49
  51.2 0.1 copy.13
  51.3 11.7 %cholesky.17 = f32[128,128]{1,0:T(8,128)S(1)} custom-call(f32[128,128]{1,0:T(8,128)S(1)} %fusion.24), custom_call_target="Cholesky" | custom-call | tf_op jit(solution)/shard_map/jit(cholesky)/cholesky | solution.py:54
  63.0 0.6 compare_reduce_fusion
  63.7 0.7 fusion.19
  64.4 9.8 %custom-call.10 = f32[1,128,128]{1,2,0:T(8,128)S(1)} custom-call(f32[1,128,128]{2,1,0:T(8,128)S(1)} %fusion.19), custom_call_target="InvertDiagBlocksLowerTriangular" | custom-call | tf_op jit(solution)/shard_map/jit(_cho_solve)/triangular_solve | solution.py:55
  74.2 0.2 fusion.22
  74.4 0.2 fusion.20
  74.6 1.4 %fusion.35 = f32[1024,128]{1,0:T(8,128)} fusion(f32[1024,128]{1,0:T(8,128)S(1)} %convolution_add_fusion, f32[128,128]{1,0:T(8,128)S(1)} %fusion.20), kind=kOutput, calls=%fused_computation.57 | convolution fusion | flops 201326592 | bytes 1114112 | tf_op jit(solution)/shard_map/dot_general | solution.py:58
  (12 shorter events, 0.2 us)
Async XLA Ops:
  0.0 36.4 %copy-start = (bf16[1024,128]{1,0:T(8,128)(2,1)S(1)}, bf16[1024,128]{1,0:T(8,128)(2,1)}, u32[]{:S(2)}) copy-start(bf16[1024,128]{1,0:T(8,128)(2,1)} %param.5) | copy-start | bytes 786436
  1.4 35.6 %collective-permute-start.2 = (f32[128,128]{0,1:T(8,128)S(1)}, f32[128,128]{0,1:T(8,128)S(1)}, u32[]{:S(2)}, u32[]{:S(2)}) collective-permute-start(f32[128,128]{0,1:T(8,128)S(1)} %fusion.34), channel_id=1, source_target_pairs={{0,1},{1,0},{2,3},{3,2},{4,5},{5,4},{6,7},{7,6},{8,9},{9,8},{10,11... | collective-permute-start | bytes 196616 | tf_op jit(solution)/shard_map/ppermute | solution.py:49
  2.7 33.7 %collective-permute-start = (bf16[128,128]{1,0:T(8,128)(2,1)S(1)}, bf16[128,128]{1,0:T(8,128)(2,1)S(1)}, u32[]{:S(2)}, u32[]{:S(2)}) collective-permute-start(bf16[128,128]{1,0:T(8,128)(2,1)S(1)} %get-tuple-element.11), channel_id=1, source_target_pairs={{0,1},{1,2},{2,3},{3,4},{4,5},{5,6},{6,7},{7,8},{8,9},{9,10},{10,1... | collective-permute-start | bytes 98312 | tf_op jit(solution)/shard_map/ppermute | solution.py:17
  4.6 32.3 %collective-permute-start.1 = (bf16[128,128]{1,0:T(8,128)(2,1)S(1)}, bf16[128,128]{1,0:T(8,128)(2,1)S(1)}, u32[]{:S(2)}, u32[]{:S(2)}) collective-permute-start(bf16[128,128]{1,0:T(8,128)(2,1)S(1)} %get-tuple-element.12), channel_id=1, source_target_pairs={{1,0},{2,1},{3,2},{4,3},{5,4},{6,5},{7,6},{8,7},{9,8},{10,9},{11,1... | collective-permute-start | bytes 98312 | tf_op jit(solution)/shard_map/ppermute | solution.py:18
  9.7 26.8 %copy-start.1 = (bf16[16,5,64,64]{3,2,1,0:T(8,128)(2,1)S(1)}, bf16[16,5,64,64]{3,2,1,0:T(8,128)(2,1)}, u32[]{:S(2)}) copy-start(bf16[16,5,64,64]{3,2,1,0:T(8,128)(2,1)} %param.6) | copy-start | bytes 1966084
  37.0 4.4 %collective-permute-start.3 = (f32[128,128]{0,1:T(8,128)S(1)}, f32[128,128]{0,1:T(8,128)S(1)}, u32[]{:S(2)}, u32[]{:S(2)}) collective-permute-start(f32[128,128]{0,1:T(8,128)S(1)} %add.87), channel_id=1, source_target_pairs={{0,2},{1,3},{2,0},{3,1},{4,6},{5,7},{6,4},{7,5},{8,10},{9,11},{10,... | collective-permute-start | bytes 196616 | tf_op jit(solution)/shard_map/ppermute | solution.py:49
  37.3 8.6 %copy-start.2 = (bf16[1024,512]{1,0:T(8,128)(2,1)S(1)}, bf16[1024,512]{1,0:T(8,128)(2,1)}, u32[]{:S(2)}) copy-start(bf16[1024,512]{1,0:T(8,128)(2,1)} %param.7) | copy-start | bytes 3145732
  41.5 4.3 %collective-permute-start.4 = (f32[128,128]{0,1:T(8,128)S(1)}, f32[128,128]{0,1:T(8,128)S(1)}, u32[]{:S(2)}, u32[]{:S(2)}) collective-permute-start(f32[128,128]{0,1:T(8,128)S(1)} %add.88), channel_id=1, source_target_pairs={{0,4},{1,5},{2,6},{3,7},{4,0},{5,1},{6,2},{7,3},{8,12},{9,13},{10,... | collective-permute-start | bytes 196616 | tf_op jit(solution)/shard_map/ppermute | solution.py:49
  45.8 5.4 %collective-permute-start.5 = (f32[128,128]{0,1:T(8,128)S(1)}, f32[128,128]{0,1:T(8,128)S(1)}, u32[]{:S(2)}, u32[]{:S(2)}) collective-permute-start(f32[128,128]{0,1:T(8,128)S(1)} %add.89), channel_id=1, source_target_pairs={{0,8},{1,9},{2,10},{3,11},{4,12},{5,13},{6,14},{7,15},{8,0},{9,1},... | collective-permute-start | bytes 196616 | tf_op jit(solution)/shard_map/ppermute | solution.py:49
